TPU v7x, 32 devices: a whole 2x2x4 slice. The times are simulated.
32 devices in a mesh: bpar: 2 (over y), tgt: 4 (over z), prj: 2 (over x), rep: 2 (over core).
Axes of the slice: x: 2, y: 2, z: 4, core: 2. Of those that a mesh axis runs over, the one named last changes fastest.
Arguments:
- tgt_basis: bfloat16 [2, 4096, 512], P(None, 'tgt', 'rep'), may hold values from -6 to 6
- proj_basis: bfloat16 [2, 8, 512, 512], P(None, None, 'prj', 'rep'), may hold values from -0.00390625 to 0.00390625
- quad_weight: float32 [1024], P(('bpar', 'rep')), parts along dimension 0, may hold values from 0.3 to 3
- tgt_energy: float32 [4096], P(('tgt', 'prj', 'rep')), may hold values from -1 to 1
- proj_energy: float32 [8, 512], P(('tgt', 'rep'), 'prj'), may hold values from -1 to 1
- pair_flags: int32 [8, 2], P('bpar'), parts along dimension 0, may hold values 0 or 1
- tile_counts: int32 [8, 2], P('bpar'), parts along dimension 0, may hold values from 1 to 4
- tgt_amp: float32 [8192, 128], P(('bpar', 'tgt', 'prj', 'rep')), parts along dimension 0, may hold values from -6 to 6
- proj_amp: float32 [16, 512, 128], P(('bpar', 'tgt', 'rep'), 'prj'), parts along dimension 0, may hold values from -6 to 6
Outputs:
- new_tgt_amp: float32 [8192, 128], P(('bpar', 'tgt', 'prj', 'rep')), parts along dimension 0
- new_proj_amp: float32 [16, 512, 128], P(('bpar', 'tgt', 'rep'), 'prj'), parts along dimension 0
There are 2 independent parts, one for each index of `bpar`. A program takes and returns all parts, laid end to end along the dimension named above; an argument that names none is the same for every part. Nothing has to cross between parts.
All inputs are finite; a program needn't handle non-finite values.
Results may differ from a plain program's by a relative error of at most 0.02.
Values may be sent and summed in bfloat16 or wider, within the bound.
A program may use at most 64 MiB of HBM per device.

v0:
```python
import jax
import jax.numpy as jnp
from jax import lax
from jax.sharding import PartitionSpec as P

time_step = 0.4


def rotate(energy, state_now, coupled):
    half_cols = state_now.shape[-1] // 2
    summed = energy[..., None] * state_now + coupled
    return jnp.concatenate([summed[..., half_cols:], -summed[..., :half_cols]], axis=-1)


def turned(amplitude):
    half_cols = amplitude.shape[-1] // 2
    return jnp.concatenate([amplitude[..., half_cols:], -amplitude[..., :half_cols]], axis=-1)


def conj_project(basis_real, basis_imag, amplitude):
    contract = (((0,), (0,)), ((), ()))
    first_part = lax.dot_general(
        basis_real, amplitude, contract, preferred_element_type=jnp.float32
    )
    second = lax.dot_general(
        basis_imag, turned(amplitude), contract, preferred_element_type=jnp.float32
    )
    return first_part + second


def expand(basis_real, basis_imag, projected):
    first_part = jnp.dot(basis_real, projected, preferred_element_type=jnp.float32)
    second = jnp.dot(basis_imag, turned(projected), preferred_element_type=jnp.float32)
    return first_part - second


def shards(
    tgt_basis,
    proj_basis,
    quad_weight,
    tgt_energy,
    proj_energy,
    pair_flags,
    tile_counts,
    tgt_amp,
    proj_amp,
):
    rep_index = lax.axis_index("rep")
    tgt_index = lax.axis_index("tgt")
    prj_index = lax.axis_index("prj")
    pair_flag = pair_flags[tgt_index, prj_index]
    pair_tiles = tile_counts[tgt_index, prj_index]
    tile_width = quad_weight.shape[0] // 2
    lower_tiles = (
        tgt_basis[..., :tile_width],
        proj_basis[..., :tile_width],
        quad_weight[:tile_width],
    )
    upper_tiles = (
        tgt_basis[..., tile_width:],
        proj_basis[..., tile_width:],
        quad_weight[tile_width:],
    )
    first_tiles = list(lower_tiles)
    second_tiles = list(upper_tiles)
    tile_ids = (2 * rep_index, 2 * rep_index + 1)
    slot_list = []
    for tile_id, tile_set in zip(tile_ids, (first_tiles, second_tiles)):
        is_live = jnp.logical_and(pair_flag > 0, tile_id < pair_tiles)
        slot_list.append((is_live, tile_set[0], tile_set[1], tile_set[2]))

    def coupled_rates(tgt_state, proj_state):
        tgt_send = tgt_state.astype(jnp.bfloat16)
        proj_send = proj_state.astype(jnp.bfloat16)
        two_cols = tgt_state.shape[-1]
        group_rows = proj_state.shape[1]
        zero_block = jnp.zeros((tile_width, two_cols), jnp.float32)
        shard_rows = lax.all_gather(tgt_send, ("prj", "rep"), axis=0, tiled=True)
        row_count = shard_rows.shape[0]
        updated = []
        for add_slot_index in range(2):
            is_live, tgt_tile = (slot_list[add_slot_index][0], slot_list[add_slot_index][1])
            basis_real = tgt_tile[0]
            basis_imag = tgt_tile[1]
            term = lax.cond(
                is_live,
                lambda: conj_project(basis_real, basis_imag, shard_rows),
                lambda: zero_block,
            )
            updated.append(term)
        tgt_raw = (updated[0], updated[1])
        target_coefficient = [
            (slot_list[slot_index][3][:, None] * tgt_raw[slot_index]).astype(jnp.bfloat16)
            for slot_index in range(2)
        ]

        def add_projectile(shard_rows):
            row_count = shard_rows.shape[0]
            flat_rows = shard_rows.reshape(row_count * group_rows, two_cols)
            updated = []
            for slot_index in range(2):
                is_live, proj_tile = (slot_list[slot_index][0], slot_list[slot_index][2])
                basis_real = proj_tile[0].reshape(row_count * group_rows, tile_width)
                basis_imag = proj_tile[1].reshape(row_count * group_rows, tile_width)
                term = lax.cond(
                    is_live,
                    lambda: conj_project(basis_real, basis_imag, flat_rows),
                    lambda: zero_block,
                )
                updated.append(term)
            return (updated[0], updated[1])

        proj_raw = add_projectile(lax.all_gather(proj_send, ("tgt", "rep"), axis=0, tiled=True))
        projectile_coefficient = [
            (slot_list[slot_index][3][:, None] * proj_raw[slot_index]).astype(jnp.bfloat16)
            for slot_index in range(2)
        ]
        row_count = proj_state.shape[0] * lax.axis_size(("tgt", "rep"))
        zero_terms = jnp.zeros((row_count, group_rows, two_cols), jnp.float32)
        summed = zero_terms
        for slot_index in range(2):
            is_live, proj_tile = (slot_list[slot_index][0], slot_list[slot_index][2])
            projectile_basis_real = proj_tile[0].reshape(row_count * group_rows, tile_width)
            projectile_basis_imag = proj_tile[1].reshape(row_count * group_rows, tile_width)
            coef_now = target_coefficient[slot_index]
            term = lax.cond(
                is_live,
                lambda: expand(projectile_basis_real, projectile_basis_imag, coef_now).reshape(
                    row_count, group_rows, two_cols
                ),
                lambda: zero_terms,
            )
            summed = summed + term
        proj_coupled = lax.psum_scatter(
            summed.astype(jnp.bfloat16), ("tgt", "rep"), scatter_dimension=0, tiled=True
        ).astype(jnp.float32)
        target_zero_terms = jnp.zeros(
            (tgt_state.shape[0] * lax.axis_size(("prj", "rep")), two_cols), jnp.float32
        )
        summed = target_zero_terms
        for slot_index in range(2):
            is_live, tgt_tile = (slot_list[slot_index][0], slot_list[slot_index][1])
            target_basis_real = tgt_tile[0]
            target_basis_imag = tgt_tile[1]
            target_coef_now = projectile_coefficient[slot_index]
            term = lax.cond(
                is_live,
                lambda: expand(target_basis_real, target_basis_imag, target_coef_now),
                lambda: target_zero_terms,
            )
            summed = summed + term
        tgt_coupled = lax.psum_scatter(
            summed.astype(jnp.bfloat16), ("prj", "rep"), scatter_dimension=0, tiled=True
        ).astype(jnp.float32)
        return (
            rotate(tgt_energy, tgt_state, tgt_coupled),
            rotate(proj_energy, proj_state, proj_coupled),
        )

    tgt_rate, proj_rate = coupled_rates(tgt_amp, proj_amp)
    tgt_half = tgt_amp + 0.5 * time_step * tgt_rate
    proj_half = proj_amp + 0.5 * time_step * proj_rate
    tgt_rate, proj_rate = coupled_rates(tgt_half, proj_half)
    return (tgt_amp + time_step * tgt_rate, proj_amp + time_step * proj_rate)


def solution(mesh):
    in_specs = (
        P(None, "tgt", "rep"),
        P(None, None, "prj", "rep"),
        P(("bpar", "rep")),
        P(("tgt", "prj", "rep")),
        P(("tgt", "rep"), "prj"),
        P("bpar", None),
        P("bpar", None),
        P(("bpar", "tgt", "prj", "rep"), None),
        P(("bpar", "tgt", "rep"), "prj", None),
    )
    out_specs = (P(("bpar", "tgt", "prj", "rep"), None), P(("bpar", "tgt", "rep"), "prj", None))
    return jax.shard_map(shards, mesh=mesh, in_specs=in_specs, out_specs=out_specs, check_vma=False)
```

profile of v0, /device:TPU:1, one launch (start us, length us, event | category | flops | bytes accessed | tf_op | source)
XLA Modules:
  0.0 207.5 jit_solution(11372533353395268817)
XLA Ops:
  7.2 0.0 reduce-scatter.5.cloned.1.call-start
  7.2 1.3 dynamic_slice.6
  8.5 1.3 dynamic_slice.7
  11.2 2.1 %slice_bitcast_fusion = (bf16[1024,128]{1,0:T(8,128)(2,1)S(1)}, bf16[1024,128]{1,0:T(8,128)(2,1)}, bf16[1024,128]{1,0:T(8,128)(2,1)S(1)}, bf16[1024,128]{1,0:T(8,128)(2,1)S(1)}) fusion(bf16[2,1024,256]{2,1,0:T(8,128)(2,1)} %param.41), kind=kLoop, calls=%fused_computation.116 | loop fusion | bytes 2097152 | tf_op jit(solution)/shard_map/squeeze | solution.py:144
  13.3 0.6 fusion.102
  14.6 16.5 %all_gather.12 = bf16[8,256,128]{2,1,0:T(8,128)(2,1)S(1)} all-gather(bf16[1,256,128]{2,1,0:T(8,128)(2,1)S(1)} %convert_element_type.81), channel_id=1, replica_groups=mesh['bpar'=2,'tgt'=4,'prj'=2,'rep'=2] {'tgt','rep'}, dimensions={0}, use_global_device_ids=true | all-gather | bytes 589824 | tf_op jit(solution)/shard_map/all_gather | solution.py:113
  31.1 0.6 conditional.16
  31.1 0.6 broadcast.52
  31.7 1.5 multiply_convert_fusion.7
  33.2 0.8 conditional.17
  33.2 0.8 broadcast.53
  34.1 0.6 conditional.18
  34.1 0.6 broadcast.54
  34.7 1.6 multiply_convert_fusion.6
  36.3 0.8 conditional.19
  36.3 0.8 broadcast.55
  37.1 1.8 add_convert_fusion.3
  38.9 0.0 reduce-scatter.5.cloned.1.call-update
  39.0 0.0 reduce-scatter.7.cloned.1.call-start
  39.0 28.0 %reduce-scatter.5.cloned.1.call-done = bf16[256,128]{1,0:T(8,128)(2,1)} async-done(((bf16[1024,128]{1,0:T(8,128)(2,1)}), bf16[256,128]{1,0:T(8,128)(2,1)}) %reduce-scatter.5.cloned.1.call-update) | async-done | bytes 65552 | tf_op jit(solution)/shard_map/reduce_scatter | solution.py:152
  67.0 1.0 convert_add_fusion.3
  68.1 0.1 fusion.105
  68.2 1.2 fusion.85
  69.4 6.4 %all_gather.13 = bf16[1024,128]{1,0:T(8,128)(2,1)S(1)} all-gather(bf16[256,128]{1,0:T(8,128)(2,1)S(1)} %get-tuple-element.239), channel_id=1, replica_groups=mesh['bpar'=2,'tgt'=4,'prj'=2,'rep'=2] {'prj','rep'}, dimensions={0}, use_global_device_ids=true | all-gather | bytes 327680 | tf_op jit(solution)/shard_map/all_gather | solution.py:78
  75.8 5.9 %all_gather.15 = bf16[1024,128]{1,0:T(8,128)(2,1)S(1)} all-gather(bf16[256,128]{1,0:T(8,128)(2,1)S(1)} %get-tuple-element.238), channel_id=1, replica_groups=mesh['bpar'=2,'tgt'=4,'prj'=2,'rep'=2] {'prj','rep'}, dimensions={0}, use_global_device_ids=true | all-gather | bytes 327680 | tf_op jit(solution)/shard_map/all_gather | solution.py:78
  81.6 0.6 conditional.30
  81.6 0.6 broadcast.66
  82.2 0.6 conditional.22
  82.2 0.6 broadcast.58
  82.9 0.6 copy-done.10
  83.5 0.6 conditional.28
  83.5 0.6 broadcast.64
  84.1 1.0 multiply_convert_fusion
  85.2 1.1 conditional.21
  85.2 1.1 broadcast.57
  86.3 1.1 conditional.23
  86.3 1.1 broadcast.59
  87.4 2.4 %add_convert_fusion.1 = bf16[8,256,128]{2,1,0:T(8,128)(2,1)} fusion(f32[8,256,128]{2,1,0:T(8,128)} %get-tuple-element.259, f32[8,256,128]{2,1,0:T(8,128)} %get-tuple-element.261), kind=kLoop, calls=%fused_computation.113 | loop fusion | flops 524288 | bytes 2621440 | tf_op jit(solution)/shard_map/convert_element_type | solution.py:135
  89.8 0.0 reduce-scatter.11.cloned.1.call-start
  89.9 1.1 conditional.29
  89.9 1.1 broadcast.65
  91.0 1.1 conditional.31
  91.0 1.1 broadcast.67
  92.1 2.4 %add_convert_fusion = bf16[8,256,128]{2,1,0:T(8,128)(2,1)} fusion(f32[8,256,128]{2,1,0:T(8,128)} %get-tuple-element.267, f32[8,256,128]{2,1,0:T(8,128)} %get-tuple-element.269), kind=kLoop, calls=%fused_computation.112 | loop fusion | flops 524288 | bytes 2621440 | tf_op jit(solution)/shard_map/convert_element_type | solution.py:135
  94.6 0.0 reduce-scatter.9.cloned.1.call-start
  94.6 28.7 %reduce-scatter.7.cloned.1.call-done = bf16[1,256,128]{2,1,0:T(8,128)(2,1)} async-done(((bf16[8,256,128]{2,1,0:T(8,128)(2,1)}), bf16[1,256,128]{2,1,0:T(8,128)(2,1)}) %reduce-scatter.7.cloned.1.call-update) | async-done | bytes 65552 | tf_op jit(solution)/shard_map/reduce_scatter | solution.py:134
  123.3 0.9 convert_add_fusion.2
  124.2 0.1 fusion.106
  124.3 30.4 %reduce-scatter.11.cloned.1.call-done = bf16[1,256,128]{2,1,0:T(8,128)(2,1)} async-done(((bf16[8,256,128]{2,1,0:T(8,128)(2,1)}), bf16[1,256,128]{2,1,0:T(8,128)(2,1)}) %reduce-scatter.11.cloned.1.call-update) | async-done | bytes 65552 | tf_op jit(solution)/shard_map/reduce_scatter | solution.py:134
  154.7 1.6 convert_add_fusion
  156.4 18.9 %all_gather.14 = bf16[8,256,128]{2,1,0:T(8,128)(2,1)S(1)} all-gather(bf16[1,256,128]{2,1,0:T(8,128)(2,1)S(1)} %get-tuple-element.235), channel_id=1, replica_groups=mesh['bpar'=2,'tgt'=4,'prj'=2,'rep'=2] {'tgt','rep'}, dimensions={0}, use_global_device_ids=true | all-gather | bytes 589824 | tf_op jit(solution)/shard_map/all_gather | solution.py:113
  175.3 0.6 conditional.24
  175.3 0.6 broadcast.60
  175.9 0.9 multiply_convert_fusion.3
  176.9 0.1 multiply_convert_fusion.2
  177.0 0.8 copy-done
  177.9 0.1 conditional.27
  178.0 0.8 add_convert_fusion.2
  178.8 0.1 fusion.103
  178.9 0.8 fusion.83
  179.6 19.5 %reduce-scatter.9.cloned.1.call-done = bf16[256,128]{1,0:T(8,128)(2,1)} async-done(((bf16[1024,128]{1,0:T(8,128)(2,1)}), bf16[256,128]{1,0:T(8,128)(2,1)}) %reduce-scatter.9.cloned.1.call-update) | async-done | bytes 65552 | tf_op jit(solution)/shard_map/reduce_scatter | solution.py:152
  199.1 1.0 convert_add_fusion.1
  200.1 0.1 fusion.104
  200.2 0.8 fusion.82
  (38 shorter events, 0.3 us)
Async XLA Ops:
  7.2 59.9 %reduce-scatter.5.cloned.1.call-start = ((), (), s32[]{:S(2)}) async-start(), calls=%async_computation.4 | async-start | bytes 327680 | tf_op jit(solution)/shard_map/reduce_scatter | solution.py:152
  11.1 2.1 %copy-start.1 = (bf16[2,8,256,256]{3,2,1,0:T(8,128)(2,1)S(1)}, bf16[2,8,256,256]{3,2,1,0:T(8,128)(2,1)}, u32[]{:S(2)}) copy-start(bf16[2,8,256,256]{3,2,1,0:T(8,128)(2,1)} %param.42) | copy-start | bytes 6291460
  13.3 1.3 copy-start.3
  13.3 17.8 %copy-start.13 = (f32[256]{0:T(256)S(1)}, f32[256]{0:T(256)}, u32[]{:S(2)}) copy-start(f32[256]{0:T(256)} %param.43) | copy-start | bytes 3076
  34.7 2.4 %copy-start.2 = (f32[1024,128]{1,0:T(8,128)S(1)}, f32[1024,128]{1,0:T(8,128)}, u32[]{:S(2)}) copy-start(f32[1024,128]{1,0:T(8,128)} %get-tuple-element.255) | copy-start | bytes 1572868
  36.3 30.7 %copy-start.12 = (f32[256]{0:T(256)S(1)}, f32[256]{0:T(256)}, u32[]{:S(2)}) copy-start(f32[256]{0:T(256)} %param.44) | copy-start | bytes 3076
  39.0 84.3 %reduce-scatter.7.cloned.1.call-start = ((), (), s32[]{:S(2)}) async-start(), calls=%async_computation.5 | async-start | bytes 589824 | tf_op jit(solution)/shard_map/reduce_scatter | solution.py:134
  68.2 7.6 %copy-start.6 = (f32[256,64]{1,0:T(8,128)}, f32[256,64]{1,0:T(8,128)S(1)}, u32[]{:S(2)}) copy-start(f32[256,64]{1,0:T(8,128)S(1)} %get-tuple-element.242) | copy-start | bytes 196612
  68.2 7.6 %copy-start.8 = (f32[256,64]{1,0:T(8,128)}, f32[256,64]{1,0:T(8,128)S(1)}, u32[]{:S(2)}) copy-start(f32[256,64]{1,0:T(8,128)S(1)} %get-tuple-element.243) | copy-start | bytes 196612
  82.9 0.6 copy-start.10
  89.8 64.9 %reduce-scatter.11.cloned.1.call-start = ((), (), s32[]{:S(2)}) async-start(), calls=%async_computation.7 | async-start | bytes 589824 | tf_op jit(solution)/shard_map/reduce_scatter | solution.py:134
  92.1 31.2 %copy-start.11 = (f32[1,256]{1,0:T(1,128)S(1)}, f32[1,256]{1,0:T(1,128)}, u32[]{:S(2)}) copy-start(f32[1,256]{1,0:T(1,128)} %param.45) | copy-start | bytes 3076
  94.6 104.5 %reduce-scatter.9.cloned.1.call-start = ((), (), s32[]{:S(2)}) async-start(), calls=%async_computation.6 | async-start | bytes 327680 | tf_op jit(solution)/shard_map/reduce_scatter | solution.py:152
  176.8 1.0 copy-start
  177.8 0.9 copy-start.5
  177.9 21.3 %copy-start.4 = (f32[256,128]{1,0:T(8,128)S(1)}, f32[256,128]{1,0:T(8,128)}, u32[]{:S(2)}) copy-start(f32[256,128]{1,0:T(8,128)} %param.48) | copy-start | bytes 393220
  177.9 21.2 %copy-start.7 = (f32[256,64]{1,0:T(8,128)S(1)}, f32[256,64]{1,0:T(8,128)}, u32[]{:S(2)}) copy-start(f32[256,64]{1,0:T(8,128)} %copy-done.6) | copy-start | bytes 196612
  177.9 21.2 %copy-start.9 = (f32[256,64]{1,0:T(8,128)S(1)}, f32[256,64]{1,0:T(8,128)}, u32[]{:S(2)}) copy-start(f32[256,64]{1,0:T(8,128)} %copy-done.8) | copy-start | bytes 196612
Sparse Core Ops, SparseCore 0:
  39.1 27.8 reduce-scatter.4
  90.0 33.2 reduce-scatter.6
  125.5 29.1 reduce-scatter.10
  178.9 20.1 reduce-scatter.8
where the time goes:
time: 208 us; the launch traced here: 207 us
  waiting for transfers between devices  107 us (51%)
  blocking collectives  47.6 us (23%)
  other arithmetic  20.3 us (10%)
  local copies, waits for them, and re-layouts  16.7 us (8%)
  between operations  16 us (8%)
    reduce_scatter x2, waiting for transfers between devices, coupled_rates(): lax.psum_scatter(summed.astype(jnp.bfloat16), ('tgt', 'rep'), scatter_dim...  59.1 us
    reduce_scatter x2, waiting for transfers between devices, coupled_rates(): lax.psum_scatter(summed.astype(jnp.bfloat16), ('prj', 'rep'), scatter_dim...  47.5 us
    all_gather x2, blocking collectives, coupled_rates(): lax.all_gather(proj_send, ('tgt', 'rep'), axis=0, tiled=True)  35.4 us
    all_gather x2, blocking collectives, coupled_rates(): shard_rows = lax.all_gather(tgt_send, ('prj', 'rep'), axis=0, tiled=True)  12.2 us
    another operation x16, local copies, waits for them, and re-layouts  9.9 us
    convert_element_type x4, other arithmetic, coupled_rates(): summed.astype(jnp.bfloat16)  7.47 us
    add x4, other arithmetic, rotate(): summed = energy[..., None] * state_now + coupled  4.58 us
  transfers between devices with their start and end apart: 4, of which 4 were waited for; matrix products, arithmetic and copies ran while one was open for 3% of the time, Pallas kernels for 0%

commit v1 on v0

--- a/solution.py
+++ b/solution.py
@@ -1,6 +1,10 @@
+import functools
+
 import jax
 import jax.numpy as jnp
 from jax import lax
+from jax.experimental import pallas as pl
+from jax.experimental.pallas import tpu as pltpu
 from jax.sharding import PartitionSpec as P
 
 time_step = 0.4
@@ -164,6 +168,352 @@
     return (tgt_amp + time_step * tgt_rate, proj_amp + time_step * proj_rate)
 
 
+def half_turn(values):
+    half = values.shape[0] // 2
+    return jnp.concatenate([values[half:], -values[:half]], axis=0)
+
+
+def step_kernel(
+    n_tgt,
+    n_prj,
+    tgt_basis,
+    proj_basis,
+    quad_weight,
+    tgt_energy,
+    proj_energy,
+    flags,
+    counts,
+    tgt_amp,
+    proj_amp,
+    tgt_out,
+    proj_out,
+    tgt_tiles,
+    proj_tiles,
+    weight,
+    energy,
+    raw,
+    state,
+    masked,
+    z_send,
+    z_recv,
+    f_send,
+    f_recv,
+    y_send,
+    y_recv,
+    load_sem,
+    init_send_sem,
+    init_recv_sem,
+    z_send_sem,
+    z_recv_sem,
+    f_send_sem,
+    f_recv_sem,
+    y_send_sem,
+    y_recv_sem,
+):
+    n = n_tgt * n_prj
+    a, b, r = lax.axis_index("tgt"), lax.axis_index("prj"), lax.axis_index("rep")
+    me = a * n_prj + b
+    rows = tgt_amp.shape[0]
+    points = quad_weight.shape[1]
+    two_cols = tgt_amp.shape[1]
+    deltas = [(da, db) for da in range(n_tgt) for db in range(n_prj)]
+    core = {"rep": 1 - r}
+
+    def chip(delta):
+        return {"tgt": lax.bitwise_xor(a, delta[0]), "prj": lax.bitwise_xor(b, delta[1])}
+
+    def chip_index(delta):
+        return lax.bitwise_xor(a, delta[0]) * n_prj + lax.bitwise_xor(b, delta[1])
+
+    loads = [
+        pltpu.make_async_copy(tgt_amp, raw.at[0, 0], load_sem.at[0]),
+        pltpu.make_async_copy(proj_amp.at[0], raw.at[1, 0], load_sem.at[1]),
+        pltpu.make_async_copy(tgt_energy, energy.at[0, 0], load_sem.at[2]),
+        pltpu.make_async_copy(proj_energy, energy.at[1, 0], load_sem.at[3]),
+        pltpu.make_async_copy(quad_weight, weight, load_sem.at[4]),
+    ]
+    for half in range(2):
+        own = r if half == 0 else 1 - r
+        start = pl.multiple_of((b * 2 + own) * rows, rows)
+        loads.append(
+            pltpu.make_async_copy(
+                tgt_basis.at[:, pl.ds(start, rows), :], tgt_tiles.at[:, half], load_sem.at[5 + half]
+            )
+        )
+        loads.append(
+            pltpu.make_async_copy(
+                proj_basis.at[:, a * 2 + own], proj_tiles.at[:, half], load_sem.at[7 + half]
+            )
+        )
+    for load in loads:
+        load.start()
+
+    barrier = pltpu.get_barrier_semaphore()
+    pl.semaphore_signal(barrier, inc=1, device_id=core, device_id_type=pl.DeviceIdType.MESH)
+    for delta in deltas[1:]:
+        pl.semaphore_signal(
+            barrier, inc=1, device_id=chip(delta), device_id_type=pl.DeviceIdType.MESH
+        )
+
+    for load in loads[:5]:
+        load.wait()
+    lane = lax.broadcasted_iota(jnp.int32, (1, points), 1)
+    tile = 2 * r + lane // (points // 2)
+    for d, delta in enumerate(deltas):
+        at = chip(delta)
+        live = jnp.logical_and(
+            tile < counts[at["tgt"], at["prj"]], flags[at["tgt"], at["prj"]] > 0
+        )
+        masked[d] = jnp.where(live, weight[...], 0.0)
+    for x in range(2):
+        state[x, 0] = raw[x, 0].T
+
+    pl.semaphore_wait(barrier, n)
+
+    def remote(src, dst, send_sem, recv_sem, device):
+        copy = pltpu.make_async_remote_copy(
+            src_ref=src,
+            dst_ref=dst,
+            send_sem=send_sem,
+            recv_sem=recv_sem,
+            device_id=device,
+            device_id_type=pl.DeviceIdType.MESH,
+        )
+        copy.start()
+        return copy
+
+    sent = []
+    greet = []
+    for x in range(2):
+        greet.append(
+            remote(raw.at[x, 0], raw.at[x, 1], init_send_sem.at[x], init_recv_sem.at[x], core)
+        )
+    for x in range(2):
+        greet.append(
+            remote(
+                energy.at[x, 0], energy.at[x, 1], init_send_sem.at[2 + x], init_recv_sem.at[2 + x], core
+            )
+        )
+    sent += greet
+    tiles = (tgt_tiles, proj_tiles)
+    grain = two_cols // n
+
+    def project(rate, x, now):
+        total = None
+        for half in range(2):
+            amp = now[half].astype(jnp.bfloat16)
+            term = jnp.dot(
+                amp, tiles[x][0, half], preferred_element_type=jnp.float32
+            ) + jnp.dot(half_turn(amp), tiles[x][1, half], preferred_element_type=jnp.float32)
+            total = term if total is None else total + term
+        z_send[rate, x] = total.astype(jnp.bfloat16).reshape(n, grain, points)
+        copies = []
+        for d, delta in enumerate(deltas[1:]):
+            copies.append(
+                remote(
+                    z_send.at[rate, x, chip_index(delta)],
+                    z_recv.at[rate, x, d],
+                    z_send_sem.at[rate, x, d],
+                    z_recv_sem.at[rate, x, d],
+                    chip(delta),
+                )
+            )
+        sent.extend(copies)
+        return copies
+
+    def combine(rate, x, copies):
+        for copy in copies:
+            copy.wait_recv()
+
+        def part(delta):
+            d = deltas.index(delta)
+            block = z_send[rate, x, me] if d == 0 else z_recv[rate, x, d - 1]
+            return block.astype(jnp.float32)
+
+        if x == 0:
+            sums = [
+                functools.reduce(jnp.add, [part((da, db)) for db in range(n_prj)])
+                for da in range(n_tgt)
+            ]
+            fields = [
+                functools.reduce(
+                    jnp.add, [masked[deltas.index((da, eb))] * sums[da] for da in range(n_tgt)]
+                )
+                for eb in range(n_prj)
+            ]
+        else:
+            sums = [
+                functools.reduce(jnp.add, [part((da, db)) for da in range(n_tgt)])
+                for db in range(n_prj)
+            ]
+            fields = [
+                functools.reduce(
+                    jnp.add, [masked[deltas.index((ea, db))] * sums[db] for db in range(n_prj)]
+                )
+                for ea in range(n_tgt)
+            ]
+        for e, field in enumerate(fields):
+            f_send[rate, x, e] = field.astype(jnp.bfloat16)
+        f_recv[rate, x, me] = fields[0].astype(jnp.bfloat16)
+        replies = []
+        for d, delta in enumerate(deltas[1:]):
+            e = delta[1] if x == 0 else delta[0]
+            replies.append(
+                remote(
+                    f_send.at[rate, x, e],
+                    f_recv.at[rate, x, me],
+                    f_send_sem.at[rate, x, d],
+                    f_recv_sem.at[rate, x, d],
+                    chip(delta),
+                )
+            )
+        sent.extend(replies)
+        return replies
+
+    def expand_rows(rate, x, replies):
+        for copy in replies:
+            copy.wait_recv()
+        other = tiles[1 - x]
+        field = f_recv[rate, x].reshape(two_cols, points)
+        turn = half_turn(field)
+        contract = (((1,), (1,)), ((), ()))
+        mine = []
+        for half in (1, 0):
+            term = lax.dot_general(
+                field, other[0, half], contract, preferred_element_type=jnp.float32
+            ) - lax.dot_general(turn, other[1, half], contract, preferred_element_type=jnp.float32)
+            mine.insert(0, term)
+            if half == 1 or rate == 0:
+                y_send[rate, x, 1 - half] = term.astype(jnp.bfloat16)
+        if rate == 0:
+            copy = remote(
+                y_send.at[0, x], y_recv.at[0, x], y_send_sem.at[0, x], y_recv_sem.at[0, x], core
+            )
+        else:
+            copy = remote(
+                y_send.at[1, x, 0], y_recv.at[1, x, 0], y_send_sem.at[1, x], y_recv_sem.at[1, x], core
+            )
+        sent.append(copy)
+        return copy, mine
+
+    def advance(rate, x, pending, half):
+        _, mine = pending
+        c = 1 - x
+        total = mine[half] + y_recv[rate, x, half].astype(jnp.float32)
+        amp = state[c, half]
+        summed = energy[c, half] * (amp if rate == 0 else mid[c][0]) + total
+        return amp + (0.5 * time_step if rate == 0 else time_step) * half_turn(summed)
+
+    mid = [None, None]
+    loads[5].wait()
+    loads[7].wait()
+    for copy in greet:
+        copy.wait_recv()
+    loads[6].wait()
+    loads[8].wait()
+    z = [None, None]
+    for x in range(2):
+        state[x, 1] = raw[x, 1].T
+        z[x] = project(0, x, [state[x, 0], state[x, 1]])
+    f = [combine(0, x, z[x]) for x in range(2)]
+    y = [expand_rows(0, x, f[x]) for x in range(2)]
+    for x in range(2):
+        c = 1 - x
+        y[x][0].wait_recv()
+        mid[c] = [advance(0, x, y[x], half) for half in range(2)]
+        z[c] = project(1, c, mid[c])
+    f = [None, None]
+    for x in (1, 0):
+        f[x] = combine(1, x, z[x])
+    y = [None, None]
+    for x in (1, 0):
+        y[x] = expand_rows(1, x, f[x])
+    for x in (1, 0):
+        y[x][0].wait_recv()
+        new = advance(1, x, y[x], 0).T
+        if x == 1:
+            tgt_out[...] = new
+        else:
+            proj_out[0] = new
+    for copy in sent:
+        copy.wait_send()
+
+
+def kernel_shards(
+    n_tgt,
+    n_prj,
+    tgt_basis,
+    proj_basis,
+    quad_weight,
+    tgt_energy,
+    proj_energy,
+    pair_flags,
+    tile_counts,
+    tgt_amp,
+    proj_amp,
+):
+    n = n_tgt * n_prj
+    rows, two_cols = tgt_amp.shape
+    points = quad_weight.shape[0]
+    grain = two_cols // n
+    most = max(n_tgt, n_prj)
+    hbm = pl.BlockSpec(memory_space=pltpu.HBM)
+    smem = pl.BlockSpec(memory_space=pltpu.SMEM)
+    vmem = pl.BlockSpec(memory_space=pltpu.VMEM)
+    bf16, f32 = jnp.bfloat16, jnp.float32
+    dma = pltpu.SemaphoreType.DMA
+    return pl.pallas_call(
+        functools.partial(step_kernel, n_tgt, n_prj),
+        out_shape=(
+            jax.ShapeDtypeStruct(tgt_amp.shape, f32),
+            jax.ShapeDtypeStruct(proj_amp.shape, f32),
+        ),
+        in_specs=[hbm] * 5 + [smem] * 2 + [hbm] * 2,
+        out_specs=(vmem, vmem),
+        scratch_shapes=[
+            pltpu.VMEM((2, 2, rows, points), bf16),
+            pltpu.VMEM((2, 2, rows, points), bf16),
+            pltpu.VMEM((1, points), f32),
+            pltpu.VMEM((2, 2, 1, rows), f32),
+            pltpu.VMEM((2, 2, rows, two_cols), f32),
+            pltpu.VMEM((2, 2, two_cols, rows), f32),
+            pltpu.VMEM((n, 1, points), f32),
+            pltpu.VMEM((2, 2, n, grain, points), bf16),
+            pltpu.VMEM((2, 2, n - 1, grain, points), bf16),
+            pltpu.VMEM((2, 2, most, grain, points), bf16),
+            pltpu.VMEM((2, 2, n, grain, points), bf16),
+            pltpu.VMEM((2, 2, 2, two_cols, rows), bf16),
+            pltpu.VMEM((2, 2, 2, two_cols, rows), bf16),
+            dma((9,)),
+            dma((4,)),
+            dma((4,)),
+            dma((2, 2, n - 1)),
+            dma((2, 2, n - 1)),
+            dma((2, 2, n - 1)),
+            dma((2, 2, n - 1)),
+            dma((2, 2)),
+            dma((2, 2)),
+        ],
+        compiler_params=pltpu.CompilerParams(
+            collective_id=0, has_side_effects=True, vmem_limit_bytes=32 * 1024 * 1024
+        ),
+    )(
+        tgt_basis,
+        proj_basis,
+        quad_weight.reshape(1, points),
+        tgt_energy.reshape(1, rows),
+        proj_energy,
+        pair_flags,
+        tile_counts,
+        tgt_amp,
+        proj_amp,
+    )
+
+
+def power_of_two(value):
+    return value & (value - 1) == 0
+
+
 def solution(mesh):
     in_specs = (
         P(None, "tgt", "rep"),
@@ -177,4 +527,9 @@
         P(("bpar", "tgt", "rep"), "prj", None),
     )
     out_specs = (P(("bpar", "tgt", "prj", "rep"), None), P(("bpar", "tgt", "rep"), "prj", None))
-    return jax.shard_map(shards, mesh=mesh, in_specs=in_specs, out_specs=out_specs, check_vma=False)
+    n_tgt, n_prj = mesh.shape["tgt"], mesh.shape["prj"]
+    if power_of_two(n_tgt) and power_of_two(n_prj) and n_tgt * n_prj <= 8:
+        body = functools.partial(kernel_shards, n_tgt, n_prj)
+    else:
+        body = shards
+    return jax.shard_map(body, mesh=mesh, in_specs=in_specs, out_specs=out_specs, check_vma=False)

time: 208 us -> 42.2 us (0.20)
  waiting for transfers between devices: 107 us -> 0 us
  blocking collectives: 47.6 us -> 0 us
  Pallas kernels: 0 us -> 31.7 us
  other arithmetic: 20.3 us -> 0 us
  between operations: 16 us -> 0.65 us
  local copies, waits for them, and re-layouts: 16.7 us -> 9.5 us
    reduce_scatter x4 -> x0, waiting for transfers between devices: 107 us -> none  [the longest x2 59.1 us: coupled_rates(): lax.psum_scatter(summed.astype(jnp.bfloat16), ('tgt', 'rep'), scatter_dim...]
    all_gather x4 -> x0, blocking collectives: 47.6 us -> none  [the longest x2 35.4 us: coupled_rates(): lax.all_gather(proj_send, ('tgt', 'rep'), axis=0, tiled=True)]
    pallas_call x0 -> x1, Pallas kernels: none -> 31.7 us  [kernel_shards(): pl.pallas_call(functools.partial(step_kernel, n_tgt, n_prj), out_shape=(j...]
    convert_element_type x11 -> x0, other arithmetic: 13.8 us -> none  [the longest x4 7.47 us: coupled_rates(): summed.astype(jnp.bfloat16)]
    another operation x16 -> x0, local copies, waits for them, and re-layouts: 9.9 us -> none
    unnamed x28 -> x18, local copies, waits for them, and re-layouts: 1.5 us -> 9.5 us
    add x6 -> x0, other arithmetic: 6.12 us -> none  [the longest x4 4.58 us: rotate(): summed = energy[..., None] * state_now + coupled]
    dynamic_slice x2 -> x0, local copies, waits for them, and re-layouts: 2.6 us -> none  [the longest x1 1.32 us: shards(): pair_tiles = tile_counts[tgt_index, prj_index]]
  transfers between devices with their start and end apart: 4 -> 0, of which waited for: 4 -> 0; matrix products, arithmetic and copies ran while one was open for 3% -> 0% of each run, Pallas kernels for 0% -> 0%
where the time goes in v1:
time: 42.2 us; the launch traced here: 41.9 us
  Pallas kernels  31.7 us (75%)
  local copies, waits for them, and re-layouts  9.5 us (23%)
  between operations  0.65 us (2%)
    pallas_call x1, Pallas kernels, kernel_shards(): pl.pallas_call(functools.partial(step_kernel, n_tgt, n_prj), out_shape=(j...  31.7 us
    unnamed x18, local copies, waits for them, and re-layouts  9.5 us

profile of v1, /device:TPU:1, one launch (start us, length us, event | category | flops | bytes accessed | tf_op | source)
XLA Modules:
  0.0 41.9 jit_solution(11708474012117760182)
XLA Ops:
  0.6 0.8 %copy.11.flags = s32[4,2]{1,0:T(4,128)S(1)} copy(s32[4,2]{0,1:T(2,128)} %param.14) | data formatting | bytes 64 | tf_op args[5]
  1.4 0.8 %copy.12.counts = s32[4,2]{1,0:T(4,128)S(1)} copy(s32[4,2]{0,1:T(2,128)} %param.15) | data formatting | bytes 64 | tf_op args[6]
  2.2 0.0 copy-start
  2.2 1.6 %copy-done = bf16[2,8,256,256]{3,2,1,0:T(8,128)(2,1)S(1)} copy-done((bf16[2,8,256,256]{3,2,1,0:T(8,128)(2,1)S(1)}, bf16[2,8,256,256]{3,2,1,0:T(8,128)(2,1)}, u32[]{:S(2)}) %copy-start) | copy-done | bytes 2097176
  3.8 0.0 copy-start.1
  3.8 1.2 %copy-done.1 = bf16[2,1024,256]{2,1,0:T(8,128)(2,1)S(1)} copy-done((bf16[2,1024,256]{2,1,0:T(8,128)(2,1)S(1)}, bf16[2,1024,256]{2,1,0:T(8,128)(2,1)}, u32[]{:S(2)}) %copy-start.1) | copy-done | bytes 1048600
  5.0 0.0 copy-start.2
  5.0 0.9 %copy-done.2 = f32[256,128]{1,0:T(8,128)S(1)} copy-done((f32[256,128]{1,0:T(8,128)S(1)}, f32[256,128]{1,0:T(8,128)}, u32[]{:S(2)}) %copy-start.2) | copy-done | bytes 131096
  5.9 0.0 copy-start.3
  5.9 0.9 %copy-done.3 = f32[1,256,128]{2,1,0:T(8,128)S(1)} copy-done((f32[1,256,128]{2,1,0:T(8,128)S(1)}, f32[1,256,128]{2,1,0:T(8,128)}, u32[]{:S(2)}) %copy-start.3) | copy-done | bytes 131096
  6.8 0.0 copy-start.4
  6.8 0.7 %copy-done.4 = f32[256]{0:T(256)S(1)} copy-done((f32[256]{0:T(256)S(1)}, f32[256]{0:T(256)}, u32[]{:S(2)}) %copy-start.4) | copy-done | bytes 1048
  7.5 0.0 copy-start.5
  7.5 0.7 %copy-done.5 = f32[256]{0:T(256)S(1)} copy-done((f32[256]{0:T(256)S(1)}, f32[256]{0:T(256)}, u32[]{:S(2)}) %copy-start.5) | copy-done | bytes 1048
  8.1 0.0 copy-start.6
  8.1 0.7 %copy-done.6 = f32[1,256]{1,0:T(1,128)S(1)} copy-done((f32[1,256]{1,0:T(1,128)S(1)}, f32[1,256]{1,0:T(1,128)}, u32[]{:S(2)}) %copy-start.6) | copy-done | bytes 1048
  8.8 31.7 %shard_map.104 = (f32[256,128]{1,0:T(8,128)S(1)}, f32[1,256,128]{2,1,0:T(8,128)S(1)}) custom-call(bf16[2,1024,256]{2,1,0:T(8,128)(2,1)S(1)} %copy-done.1, bf16[2,8,256,256]{3,2,1,0:T(8,128)(2,1)S(1)} %copy-done, f32[1,256]{1,0:T(1,128)S(1)} %bitcast.2, f32[1,256]{1,0:T(1,128)S(1)} %bitcast.3, f32[1,256]{1,0:T(1,128)S(1)} %copy-done.6, ...), custom_call_target="tpu_custom_call" | custom-call | tf_op jit(solution)/shard_map/pallas_call | solution.py:465
  40.6 0.7 %copy.15 = f32[256,128]{1,0:T(8,128)} copy(f32[256,128]{1,0:T(8,128)S(1)} %get-tuple-element.4) | data formatting | bytes 262144
  41.2 0.7 %copy.16 = f32[1,256,128]{2,1,0:T(8,128)} copy(f32[1,256,128]{2,1,0:T(8,128)S(1)} %get-tuple-element.5) | data formatting | bytes 262144
Async XLA Ops:
  2.2 1.6 %copy-start = (bf16[2,8,256,256]{3,2,1,0:T(8,128)(2,1)S(1)}, bf16[2,8,256,256]{3,2,1,0:T(8,128)(2,1)}, u32[]{:S(2)}) copy-start(bf16[2,8,256,256]{3,2,1,0:T(8,128)(2,1)} %proj_basis.1) | copy-start | bytes 6291460
  3.8 1.2 %copy-start.1 = (bf16[2,1024,256]{2,1,0:T(8,128)(2,1)S(1)}, bf16[2,1024,256]{2,1,0:T(8,128)(2,1)}, u32[]{:S(2)}) copy-start(bf16[2,1024,256]{2,1,0:T(8,128)(2,1)} %tgt_basis.1) | copy-start | bytes 3145732
  5.0 0.9 %copy-start.2 = (f32[256,128]{1,0:T(8,128)S(1)}, f32[256,128]{1,0:T(8,128)}, u32[]{:S(2)}) copy-start(f32[256,128]{1,0:T(8,128)} %tgt_amp.1) | copy-start | bytes 393220
  5.9 0.9 %copy-start.3 = (f32[1,256,128]{2,1,0:T(8,128)S(1)}, f32[1,256,128]{2,1,0:T(8,128)}, u32[]{:S(2)}) copy-start(f32[1,256,128]{2,1,0:T(8,128)} %proj_amp.1) | copy-start | bytes 393220
  6.8 0.7 %copy-start.4 = (f32[256]{0:T(256)S(1)}, f32[256]{0:T(256)}, u32[]{:S(2)}) copy-start(f32[256]{0:T(256)} %param.11) | copy-start | bytes 3076
  7.5 0.7 %copy-start.5 = (f32[256]{0:T(256)S(1)}, f32[256]{0:T(256)}, u32[]{:S(2)}) copy-start(f32[256]{0:T(256)} %param.12) | copy-start | bytes 3076
  8.1 0.7 %copy-start.6 = (f32[1,256]{1,0:T(1,128)S(1)}, f32[1,256]{1,0:T(1,128)}, u32[]{:S(2)}) copy-start(f32[1,256]{1,0:T(1,128)} %proj_energy.1) | copy-start | bytes 3076

commit v2 on v1

--- a/solution.py
+++ b/solution.py
@@ -262,7 +262,7 @@
     for d, delta in enumerate(deltas):
         at = chip(delta)
         live = jnp.logical_and(
-            tile < counts[at["tgt"], at["prj"]], flags[at["tgt"], at["prj"]] > 0
+            tile < counts[at["prj"], at["tgt"]], flags[at["prj"], at["tgt"]] > 0
         )
         masked[d] = jnp.where(live, weight[...], 0.0)
     for x in range(2):
@@ -495,7 +495,7 @@
             dma((2, 2)),
         ],
         compiler_params=pltpu.CompilerParams(
-            collective_id=0, has_side_effects=True, vmem_limit_bytes=32 * 1024 * 1024
+            collective_id=0, has_side_effects=True, vmem_limit_bytes=63 * 1024 * 1024
         ),
     )(
         tgt_basis,
@@ -503,8 +503,8 @@
         quad_weight.reshape(1, points),
         tgt_energy.reshape(1, rows),
         proj_energy,
-        pair_flags,
-        tile_counts,
+        pair_flags.T,
+        tile_counts.T,
         tgt_amp,
         proj_amp,
     )

time: 42.2 us -> 36.2 us (0.86)
  local copies, waits for them, and re-layouts: 9.5 us -> 3.14 us
  Pallas kernels: 31.7 us -> 32.2 us
    unnamed x18 -> x2, local copies, waits for them, and re-layouts: 9.5 us -> 3.14 us
    pallas_call x1, Pallas kernels: 31.7 us -> 32.2 us  [kernel_shards(): pl.pallas_call(functools.partial(step_kernel, n_tgt, n_prj), out_shape=(j...]
where the time goes in v2:
time: 36.2 us; the launch traced here: 36 us
  Pallas kernels  32.2 us (89%)
  local copies, waits for them, and re-layouts  3.14 us (9%)
  between operations  0.64 us (2%)
    pallas_call x1, Pallas kernels, kernel_shards(): pl.pallas_call(functools.partial(step_kernel, n_tgt, n_prj), out_shape=(j...  32.2 us
    unnamed x2, local copies, waits for them, and re-layouts  3.14 us

profile of v2, /device:TPU:1, one launch (start us, length us, event | category | flops | bytes accessed | tf_op | source)
XLA Modules:
  0.0 36.0 jit_solution(14343859210383583455)
XLA Ops:
  0.6 32.2 %shard_map.104 = (f32[256,128]{1,0:T(8,128)}, f32[1,256,128]{2,1,0:T(8,128)}) custom-call(bf16[2,1024,256]{2,1,0:T(8,128)(2,1)} %tgt_basis.1, bf16[2,8,256,256]{3,2,1,0:T(8,128)(2,1)} %proj_basis.1, f32[1,256]{1,0:T(1,128)} %bitcast.4, f32[1,256]{1,0:T(1,128)} %bitcast.5, f32[1,256]{1,0:T(1,128)} %proj_energy.1, s32[2,4]{1,0:T(2,128)} %bitcast.6, ...), custom_call_target="tpu_custom_call" | custom-call | tf_op jit(solution)/shard_map/pallas_call | solution.py:465
  32.8 1.6 %copy.13 = f32[256,128]{1,0:T(8,128)} copy(f32[256,128]{1,0:T(8,128)} %get-tuple-element.4) | data formatting | bytes 262144
  34.4 1.6 %copy.14 = f32[1,256,128]{2,1,0:T(8,128)} copy(f32[1,256,128]{2,1,0:T(8,128)} %get-tuple-element.5) | data formatting | bytes 262144

commit v3 on v2

--- a/solution.py
+++ b/solution.py
@@ -298,17 +298,16 @@
     tiles = (tgt_tiles, proj_tiles)
     grain = two_cols // n
 
-    def project(rate, x, now):
-        total = None
-        for half in range(2):
-            amp = now[half].astype(jnp.bfloat16)
-            term = jnp.dot(
-                amp, tiles[x][0, half], preferred_element_type=jnp.float32
-            ) + jnp.dot(half_turn(amp), tiles[x][1, half], preferred_element_type=jnp.float32)
-            total = term if total is None else total + term
+    def project_half(x, half, now):
+        amp = now.astype(jnp.bfloat16)
+        return jnp.dot(amp, tiles[x][0, half], preferred_element_type=jnp.float32) + jnp.dot(
+            half_turn(amp), tiles[x][1, half], preferred_element_type=jnp.float32
+        )
+
+    def spread(rate, x, total):
         z_send[rate, x] = total.astype(jnp.bfloat16).reshape(n, grain, points)
         copies = []
-        for d, delta in enumerate(deltas[1:]):
+        for d, delta in reversed(list(enumerate(deltas[1:]))):
             copies.append(
                 remote(
                     z_send.at[rate, x, chip_index(delta)],
@@ -354,9 +353,8 @@
             ]
         for e, field in enumerate(fields):
             f_send[rate, x, e] = field.astype(jnp.bfloat16)
-        f_recv[rate, x, me] = fields[0].astype(jnp.bfloat16)
         replies = []
-        for d, delta in enumerate(deltas[1:]):
+        for d, delta in reversed(list(enumerate(deltas[1:]))):
             e = delta[1] if x == 0 else delta[0]
             replies.append(
                 remote(
@@ -368,6 +366,7 @@
                 )
             )
         sent.extend(replies)
+        f_recv[rate, x, me] = fields[0].astype(jnp.bfloat16)
         return replies
 
     def expand_rows(rate, x, replies):
@@ -405,23 +404,25 @@
         return amp + (0.5 * time_step if rate == 0 else time_step) * half_turn(summed)
 
     mid = [None, None]
-    loads[5].wait()
-    loads[7].wait()
-    for copy in greet:
-        copy.wait_recv()
-    loads[6].wait()
-    loads[8].wait()
     z = [None, None]
+    own = []
     for x in range(2):
+        loads[5 + x].wait()
+        own.append(project_half(x, 0, state[x, 0]))
+    for x in range(2):
+        loads[7 + x].wait()
+        greet[x].wait_recv()
         state[x, 1] = raw[x, 1].T
-        z[x] = project(0, x, [state[x, 0], state[x, 1]])
+        z[x] = spread(0, x, own[x] + project_half(x, 1, state[x, 1]))
     f = [combine(0, x, z[x]) for x in range(2)]
     y = [expand_rows(0, x, f[x]) for x in range(2)]
+    for copy in greet[2:]:
+        copy.wait_recv()
     for x in range(2):
         c = 1 - x
         y[x][0].wait_recv()
         mid[c] = [advance(0, x, y[x], half) for half in range(2)]
-        z[c] = project(1, c, mid[c])
+        z[c] = spread(1, c, project_half(c, 0, mid[c][0]) + project_half(c, 1, mid[c][1]))
     f = [None, None]
     for x in (1, 0):
         f[x] = combine(1, x, z[x])
@@ -465,8 +466,8 @@
     return pl.pallas_call(
         functools.partial(step_kernel, n_tgt, n_prj),
         out_shape=(
-            jax.ShapeDtypeStruct(tgt_amp.shape, f32),
-            jax.ShapeDtypeStruct(proj_amp.shape, f32),
+            pltpu.VMEM(tgt_amp.shape, f32),
+            pltpu.VMEM(proj_amp.shape, f32),
         ),
         in_specs=[hbm] * 5 + [smem] * 2 + [hbm] * 2,
         out_specs=(vmem, vmem),

time: 36.2 us -> 31.3 us (0.86)
  Pallas kernels: 32.2 us -> 29.2 us
  local copies, waits for them, and re-layouts: 3.14 us -> 1.31 us
    pallas_call x1, Pallas kernels: 32.2 us -> 29.2 us  [kernel_shards(): pl.pallas_call(functools.partial(step_kernel, n_tgt, n_prj), out_shape=(p...]
    unnamed x2, local copies, waits for them, and re-layouts: 3.14 us -> 1.31 us
where the time goes in v3:
time: 31.3 us; the launch traced here: 31.2 us
  Pallas kernels  29.2 us (93%)
  local copies, waits for them, and re-layouts  1.31 us (4%)
  between operations  0.64 us (2%)
    pallas_call x1, Pallas kernels, kernel_shards(): pl.pallas_call(functools.partial(step_kernel, n_tgt, n_prj), out_shape=(p...  29.2 us
    unnamed x2, local copies, waits for them, and re-layouts  1.31 us

profile of v3, /device:TPU:1, one launch (start us, length us, event | category | flops | bytes accessed | tf_op | source)
XLA Modules:
  0.0 31.2 jit_solution(3227645675723479104)
XLA Ops:
  0.6 29.2 %shard_map.104 = (f32[256,128]{1,0:T(8,128)S(1)}, f32[1,256,128]{2,1,0:T(8,128)S(1)}) custom-call(bf16[2,1024,256]{2,1,0:T(8,128)(2,1)} %tgt_basis.1, bf16[2,8,256,256]{3,2,1,0:T(8,128)(2,1)} %proj_basis.1, f32[1,256]{1,0:T(1,128)} %bitcast.4, f32[1,256]{1,0:T(1,128)} %bitcast.5, f32[1,256]{1,0:T(1,128)} %proj_energy.1, s32[2,4]{1,0:T(2,128)} %bitcast.6, ...), custom_call_target="tpu_custom_call" | custom-call | tf_op jit(solution)/shard_map/pallas_call | solution.py:466
  29.8 0.7 %copy.13 = f32[256,128]{1,0:T(8,128)} copy(f32[256,128]{1,0:T(8,128)S(1)} %get-tuple-element.2) | data formatting | bytes 262144
  30.5 0.7 %copy.14 = f32[1,256,128]{2,1,0:T(8,128)} copy(f32[1,256,128]{2,1,0:T(8,128)S(1)} %get-tuple-element.3) | data formatting | bytes 262144

commit v4 on v3

--- a/solution.py
+++ b/solution.py
@@ -284,6 +284,11 @@
 
     sent = []
     greet = []
+
+    def settle(keep):
+        while len(sent) > keep:
+            sent.pop(0).wait_send()
+
     for x in range(2):
         greet.append(
             remote(raw.at[x, 0], raw.at[x, 1], init_send_sem.at[x], init_recv_sem.at[x], core)
@@ -418,17 +423,21 @@
     y = [expand_rows(0, x, f[x]) for x in range(2)]
     for copy in greet[2:]:
         copy.wait_recv()
+    settle(2 * (n - 1) + 2)
     for x in range(2):
         c = 1 - x
         y[x][0].wait_recv()
         mid[c] = [advance(0, x, y[x], half) for half in range(2)]
         z[c] = spread(1, c, project_half(c, 0, mid[c][0]) + project_half(c, 1, mid[c][1]))
+    settle(2 * (n - 1))
     f = [None, None]
     for x in (1, 0):
         f[x] = combine(1, x, z[x])
+    settle(2 * (n - 1))
     y = [None, None]
     for x in (1, 0):
         y[x] = expand_rows(1, x, f[x])
+    settle(2)
     for x in (1, 0):
         y[x][0].wait_recv()
         new = advance(1, x, y[x], 0).T
@@ -436,8 +445,7 @@
             tgt_out[...] = new
         else:
             proj_out[0] = new
-    for copy in sent:
-        copy.wait_send()
+    settle(0)
 
 
 def kernel_shards(

time: 31.3 us -> 31.2 us (level)
  no operation moved by 1% of the time
where the time goes in v4:
time: 31.2 us; the launch traced here: 31.1 us
  Pallas kernels  29.1 us (93%)
  local copies, waits for them, and re-layouts  1.31 us (4%)
  between operations  0.64 us (2%)
    pallas_call x1, Pallas kernels, kernel_shards(): pl.pallas_call(functools.partial(step_kernel, n_tgt, n_prj), out_shape=(p...  29.1 us
    unnamed x2, local copies, waits for them, and re-layouts  1.31 us

profile of v4, /device:TPU:1, one launch (start us, length us, event | category | flops | bytes accessed | tf_op | source)
XLA Modules:
  0.0 31.1 jit_solution(15164647868020372700)
XLA Ops:
  0.6 29.1 %shard_map.104 = (f32[256,128]{1,0:T(8,128)S(1)}, f32[1,256,128]{2,1,0:T(8,128)S(1)}) custom-call(bf16[2,1024,256]{2,1,0:T(8,128)(2,1)} %tgt_basis.1, bf16[2,8,256,256]{3,2,1,0:T(8,128)(2,1)} %proj_basis.1, f32[1,256]{1,0:T(1,128)} %bitcast.4, f32[1,256]{1,0:T(1,128)} %bitcast.5, f32[1,256]{1,0:T(1,128)} %proj_energy.1, s32[2,4]{1,0:T(2,128)} %bitcast.6, ...), custom_call_target="tpu_custom_call" | custom-call | tf_op jit(solution)/shard_map/pallas_call | solution.py:474
  29.7 0.7 %copy.13 = f32[256,128]{1,0:T(8,128)} copy(f32[256,128]{1,0:T(8,128)S(1)} %get-tuple-element.2) | data formatting | bytes 262144
  30.4 0.7 %copy.14 = f32[1,256,128]{2,1,0:T(8,128)} copy(f32[1,256,128]{2,1,0:T(8,128)S(1)} %get-tuple-element.3) | data formatting | bytes 262144

commit v5 on v4

--- a/solution.py
+++ b/solution.py
@@ -192,6 +192,7 @@
     weight,
     energy,
     raw,
+    rounded,
     state,
     masked,
     z_send,
@@ -267,6 +268,7 @@
         masked[d] = jnp.where(live, weight[...], 0.0)
     for x in range(2):
         state[x, 0] = raw[x, 0].T
+        rounded[x, 0] = state[x, 0].astype(jnp.bfloat16)
 
     pl.semaphore_wait(barrier, n)
 
@@ -289,6 +291,13 @@
         while len(sent) > keep:
             sent.pop(0).wait_send()
 
+    early = [
+        remote(
+            rounded.at[x, 0], rounded.at[x, 1], init_send_sem.at[4 + x], init_recv_sem.at[4 + x], core
+        )
+        for x in range(2)
+    ]
+    sent += early
     for x in range(2):
         greet.append(
             remote(raw.at[x, 0], raw.at[x, 1], init_send_sem.at[x], init_recv_sem.at[x], core)
@@ -413,12 +422,14 @@
     own = []
     for x in range(2):
         loads[5 + x].wait()
-        own.append(project_half(x, 0, state[x, 0]))
+        own.append(project_half(x, 0, rounded[x, 0]))
     for x in range(2):
         loads[7 + x].wait()
+        early[x].wait_recv()
+        z[x] = spread(0, x, own[x] + project_half(x, 1, rounded[x, 1]))
+    for x in range(2):
         greet[x].wait_recv()
         state[x, 1] = raw[x, 1].T
-        z[x] = spread(0, x, own[x] + project_half(x, 1, state[x, 1]))
     f = [combine(0, x, z[x]) for x in range(2)]
     y = [expand_rows(0, x, f[x]) for x in range(2)]
     for copy in greet[2:]:
@@ -485,6 +496,7 @@
             pltpu.VMEM((1, points), f32),
             pltpu.VMEM((2, 2, 1, rows), f32),
             pltpu.VMEM((2, 2, rows, two_cols), f32),
+            pltpu.VMEM((2, 2, two_cols, rows), bf16),
             pltpu.VMEM((2, 2, two_cols, rows), f32),
             pltpu.VMEM((n, 1, points), f32),
             pltpu.VMEM((2, 2, n, grain, points), bf16),
@@ -494,8 +506,8 @@
             pltpu.VMEM((2, 2, 2, two_cols, rows), bf16),
             pltpu.VMEM((2, 2, 2, two_cols, rows), bf16),
             dma((9,)),
-            dma((4,)),
-            dma((4,)),
+            dma((6,)),
+            dma((6,)),
             dma((2, 2, n - 1)),
             dma((2, 2, n - 1)),
             dma((2, 2, n - 1)),

time: 31.2 us -> 31.1 us (level)
  no operation moved by 1% of the time
where the time goes in v5:
time: 31.1 us; the launch traced here: 30.9 us
  Pallas kernels  29 us (93%)
  local copies, waits for them, and re-layouts  1.31 us (4%)
  between operations  0.64 us (2%)
    pallas_call x1, Pallas kernels, kernel_shards(): pl.pallas_call(functools.partial(step_kernel, n_tgt, n_prj), out_shape=(p...  29 us
    unnamed x2, local copies, waits for them, and re-layouts  1.31 us

profile of v5, /device:TPU:1, one launch (start us, length us, event | category | flops | bytes accessed | tf_op | source)
XLA Modules:
  0.0 30.9 jit_solution(3173741677798542291)
XLA Ops:
  0.6 29.0 %shard_map.104 = (f32[256,128]{1,0:T(8,128)S(1)}, f32[1,256,128]{2,1,0:T(8,128)S(1)}) custom-call(bf16[2,1024,256]{2,1,0:T(8,128)(2,1)} %tgt_basis.1, bf16[2,8,256,256]{3,2,1,0:T(8,128)(2,1)} %proj_basis.1, f32[1,256]{1,0:T(1,128)} %bitcast.4, f32[1,256]{1,0:T(1,128)} %bitcast.5, f32[1,256]{1,0:T(1,128)} %proj_energy.1, s32[2,4]{1,0:T(2,128)} %bitcast.6, ...), custom_call_target="tpu_custom_call" | custom-call | tf_op jit(solution)/shard_map/pallas_call | solution.py:485
  29.6 0.7 %copy.13 = f32[256,128]{1,0:T(8,128)} copy(f32[256,128]{1,0:T(8,128)S(1)} %get-tuple-element.2) | data formatting | bytes 262144
  30.3 0.7 %copy.14 = f32[1,256,128]{2,1,0:T(8,128)} copy(f32[1,256,128]{2,1,0:T(8,128)S(1)} %get-tuple-element.3) | data formatting | bytes 262144

commit v6 on v5

--- a/solution.py
+++ b/solution.py
@@ -327,7 +327,7 @@
                     z_send.at[rate, x, chip_index(delta)],
                     z_recv.at[rate, x, d],
                     z_send_sem.at[rate, x, d],
-                    z_recv_sem.at[rate, x, d],
+                    z_recv_sem.at[rate, x],
                     chip(delta),
                 )
             )
@@ -335,8 +335,9 @@
         return copies
 
     def combine(rate, x, copies):
-        for copy in copies:
-            copy.wait_recv()
+        pltpu.make_async_copy(
+            z_recv.at[rate, x], z_recv.at[rate, x], z_recv_sem.at[rate, x]
+        ).wait()
 
         def part(delta):
             d = deltas.index(delta)
@@ -375,7 +376,7 @@
                     f_send.at[rate, x, e],
                     f_recv.at[rate, x, me],
                     f_send_sem.at[rate, x, d],
-                    f_recv_sem.at[rate, x, d],
+                    f_recv_sem.at[rate, x],
                     chip(delta),
                 )
             )
@@ -384,8 +385,8 @@
         return replies
 
     def expand_rows(rate, x, replies):
-        for copy in replies:
-            copy.wait_recv()
+        landed = f_recv.at[rate, x, pl.ds(0, n - 1)]
+        pltpu.make_async_copy(landed, landed, f_recv_sem.at[rate, x]).wait()
         other = tiles[1 - x]
         field = f_recv[rate, x].reshape(two_cols, points)
         turn = half_turn(field)
@@ -444,7 +445,6 @@
     f = [None, None]
     for x in (1, 0):
         f[x] = combine(1, x, z[x])
-    settle(2 * (n - 1))
     y = [None, None]
     for x in (1, 0):
         y[x] = expand_rows(1, x, f[x])
@@ -509,9 +509,9 @@
             dma((6,)),
             dma((6,)),
             dma((2, 2, n - 1)),
+            dma((2, 2)),
             dma((2, 2, n - 1)),
-            dma((2, 2, n - 1)),
-            dma((2, 2, n - 1)),
+            dma((2, 2)),
             dma((2, 2)),
             dma((2, 2)),
         ],

time: 31.1 us -> 30.7 us (0.987)
  Pallas kernels: 29 us -> 28.5 us
    pallas_call x1, Pallas kernels: 29 us -> 28.5 us  [kernel_shards(): pl.pallas_call(functools.partial(step_kernel, n_tgt, n_prj), out_shape=(p...]
where the time goes in v6:
time: 30.7 us; the launch traced here: 30.5 us
  Pallas kernels  28.5 us (93%)
  local copies, waits for them, and re-layouts  1.31 us (4%)
  between operations  0.64 us (2%)
    pallas_call x1, Pallas kernels, kernel_shards(): pl.pallas_call(functools.partial(step_kernel, n_tgt, n_prj), out_shape=(p...  28.5 us
    unnamed x2, local copies, waits for them, and re-layouts  1.31 us

profile of v6, /device:TPU:1, one launch (start us, length us, event | category | flops | bytes accessed | tf_op | source)
XLA Modules:
  0.0 30.5 jit_solution(65782023245709500)
XLA Ops:
  0.6 28.5 %shard_map.104 = (f32[256,128]{1,0:T(8,128)S(1)}, f32[1,256,128]{2,1,0:T(8,128)S(1)}) custom-call(bf16[2,1024,256]{2,1,0:T(8,128)(2,1)} %tgt_basis.1, bf16[2,8,256,256]{3,2,1,0:T(8,128)(2,1)} %proj_basis.1, f32[1,256]{1,0:T(1,128)} %bitcast.4, f32[1,256]{1,0:T(1,128)} %bitcast.5, f32[1,256]{1,0:T(1,128)} %proj_energy.1, s32[2,4]{1,0:T(2,128)} %bitcast.6, ...), custom_call_target="tpu_custom_call" | custom-call | tf_op jit(solution)/shard_map/pallas_call | solution.py:485
  29.2 0.7 %copy.13 = f32[256,128]{1,0:T(8,128)} copy(f32[256,128]{1,0:T(8,128)S(1)} %get-tuple-element.2) | data formatting | bytes 262144
  29.8 0.7 %copy.14 = f32[1,256,128]{2,1,0:T(8,128)} copy(f32[1,256,128]{2,1,0:T(8,128)S(1)} %get-tuple-element.3) | data formatting | bytes 262144
